TPU v7x, 32 devices: a whole 2x2x4 slice. The times are simulated.
32 devices in a mesh: member: 4 (over z), band: 8 (over y, x, core).
Axes of the slice: x: 2, y: 2, z: 4, core: 2. Of those that a mesh axis runs over, the one named last changes fastest.
Arguments:
- codes: int32 [64, 96, 6, 352], P('member', 'band'), may hold values from -127 to 127
- exponents: int32 [64, 96, 6], P('member', 'band'), may hold values from -8 to -4
- centers: float32 [6, 256], replicated, may hold values from -3 to 3
- widths: float32 [6], replicated, may hold values from 0.01 to 0.03
Outputs:
- smoothed: bfloat16 [96, 6, 352, 256], P('band', None, 'member')
All inputs are finite; a program needn't handle non-finite values.
Results may differ from a plain program's by a relative error of at most 0.0034.
Values may be sent and summed in bfloat16 or wider, within the bound.
A program may use at most 64 MiB of HBM per device.

v0:
```python
import math

import jax
import jax.numpy as jnp
from jax import lax
from jax.sharding import PartitionSpec as P


def extended(cells, sides, width):
    for axis, dim in sides:
        count = lax.axis_size(axis)
        ends = count - 1
        head = lax.slice_in_dim(cells, 0, width, axis=dim)
        tail = lax.slice_in_dim(cells, cells.shape[dim] - width, cells.shape[dim], axis=dim)
        cells = jnp.concatenate(
            [
                lax.ppermute(tail, axis, [(i, (i + 1) % count) for i in range(ends)]),
                cells,
                lax.ppermute(head, axis, [((i + 1) % count, i) for i in range(ends)]),
            ],
            axis=dim,
        )
    return cells


def var_density(item, center, width):
    field = item.astype(jnp.float32)
    scaled = (center[None, None, None, :] - field[:, :, :, None]) / width
    total = jnp.sum(jnp.exp(-0.5 * scaled * scaled), axis=0)
    return total / (field.shape[0] * width * math.sqrt(2.0 * math.pi))


def block_density(values, centers, widths):
    items = jnp.transpose(values, (2, 0, 1, 3))
    dens = lax.map(lambda t: var_density(t[0], t[1], t[2]), (items, centers, widths))
    return jnp.transpose(dens, (1, 0, 2, 3)).astype(jnp.bfloat16)


def shards(codes, exponents, centers, widths):
    scale = jnp.exp2(exponents.astype(jnp.float32))
    values = (codes.astype(jnp.float32) * scale[..., None]).astype(jnp.bfloat16)
    owned = lax.all_to_all(values, "member", split_axis=3, concat_axis=0, tiled=True)
    rows = owned.shape[1]
    cells = owned.shape[3]
    dens = block_density(owned, centers, widths)
    padded = extended(dens, (("member", 2), ("band", 0)), 2)
    padded = padded.astype(jnp.float32)
    lat_sum = (
        padded[0:rows]
        + padded[1 : rows + 1]
        + padded[2 : rows + 2]
        + padded[3 : rows + 3]
        + padded[4 : rows + 4]
    )
    total = (
        lat_sum[:, :, 0:cells]
        + lat_sum[:, :, 1 : cells + 1]
        + lat_sum[:, :, 2 : cells + 2]
        + lat_sum[:, :, 3 : cells + 3]
        + lat_sum[:, :, 4 : cells + 4]
    )
    return (total / 25.0).astype(jnp.bfloat16)


def solution(mesh):
    return jax.shard_map(
        shards,
        mesh=mesh,
        in_specs=(P("member", "band", None, None), P("member", "band", None), P(), P()),
        out_specs=P("band", None, "member", None),
        check_vma=False,
    )
```

profile of v0, /device:TPU:1, one launch (start us, length us, event | category | flops | bytes accessed | tf_op | source)
XLA Modules:
  0.0 257.4 jit_solution(12647910525255101593)
XLA Ops:
  0.9 1.7 multiply_convert_fusion
  2.6 13.3 %copy.15 = bf16[16,12,6,352]{0,2,1,3:T(8,128)(2,1)} copy(bf16[16,12,6,352]{3,0,2,1:T(8,128)(2,1)S(1)} %multiply_convert_fusion) | data formatting | bytes 1622016 | tf_op jit(solution)/shard_map/convert_element_type | solution.py:41
  16.0 9.2 %reshape.26 = bf16[4,2,50688]{2,1,0:T(2,128)(2,1)} reshape(bf16[352,12,6,16]{3,2,1,0:T(8,128)(2,1)} %bitcast.28) | data formatting | bytes 1622016
  25.2 5.4 %all-to-all-start = ((bf16[4,2,50688]{2,1,0:T(2,128)(2,1)}), bf16[4,2,50688]{2,1,0:T(2,128)(2,1)}, u32[]{:S(2)}, u32[]{:S(2)}) async-start(bf16[4,2,50688]{2,1,0:T(2,128)(2,1)} %reshape.26), calls=%async_computation | async-start | bytes 1622016 | tf_op jit(solution)/shard_map/all_to_all | solution.py:42
  30.6 20.2 %all-to-all-done = bf16[4,2,50688]{2,1,0:T(2,128)(2,1)} async-done(((bf16[4,2,50688]{2,1,0:T(2,128)(2,1)}), bf16[4,2,50688]{2,1,0:T(2,128)(2,1)}, u32[]{:S(2)}, u32[]{:S(2)}) %all-to-all-start) | async-done | bytes 811040 | tf_op jit(solution)/shard_map/all_to_all | solution.py:42
  50.8 10.4 %reshape.27 = bf16[352,12,6,16]{3,2,1,0:T(8,128)(2,1)} reshape(bf16[4,2,50688]{2,1,0:T(2,128)(2,1)} %all-to-all-done) | data formatting | bytes 1622016
  61.3 13.5 %copy.16 = bf16[4,16,12,6,88]{4,2,1,0,3:T(8,128)(2,1)} copy(bf16[4,16,12,6,88]{1,3,2,4,0:T(8,128)(2,1)} %bitcast.29) | data formatting | bytes 1622016 | tf_op jit(solution)/shard_map/all_to_all | solution.py:42
  74.7 132.7 %while.12 = (s32[]{:T(128)}, bf16[6,12,88,256]{3,2,0,1:T(8,128)(2,1)S(1)}, f32[6,256]{1,0:T(8,128)}, bf16[6,64,12,88]{3,2,1,0:T(8,128)(2,1)}, f32[6]{0:T(128)S(1)}, /*index=5*/s32[]{:T(128)}, f32[]{:T(128)}) while((s32[]{:T(128)}, bf16[6,12,88,256]{3,2,0,1:T(8,128)(2,1)S(1)}, f32[6,256]{1,0:T(8,128)}, bf16[6,64,12,88]{3,2,1,0:T(8,128)(2,1)}, ...), condition=%wide.region_2.3_spmd, body=%wide.region_0.2_spmd.sunk | while | flops 86575104 | bytes 3923073 | solution.py:35
  77.6 19.2 %fusion.6 = f32[12,88,256]{2,1,0:T(8,128)S(1)} fusion(f32[]{:T(128)} %bitcast.26, f32[64,12,88]{2,1,0:T(8,128)S(1)} %bitcast_convert_fusion.2, f32[256]{0:T(256)S(1)} %bitcast.34), kind=kLoop, calls=%fused_computation.2.clone.1 | loop fusion | flops 86237184 | bytes 1352708 | tf_op jit(solution)/shard_map/while/body/eval_jaxpr/reduce_sum | solution.py:29
  99.7 19.2 %fusion.6 = f32[12,88,256]{2,1,0:T(8,128)S(1)} fusion(f32[]{:T(128)} %bitcast.26, f32[64,12,88]{2,1,0:T(8,128)S(1)} %bitcast_convert_fusion.2, f32[256]{0:T(256)S(1)} %bitcast.34), kind=kLoop, calls=%fused_computation.2.clone.1 | loop fusion | flops 86237184 | bytes 1352708 | tf_op jit(solution)/shard_map/while/body/eval_jaxpr/reduce_sum | solution.py:29
  121.8 19.2 %fusion.6 = f32[12,88,256]{2,1,0:T(8,128)S(1)} fusion(f32[]{:T(128)} %bitcast.26, f32[64,12,88]{2,1,0:T(8,128)S(1)} %bitcast_convert_fusion.2, f32[256]{0:T(256)S(1)} %bitcast.34), kind=kLoop, calls=%fused_computation.2.clone.1 | loop fusion | flops 86237184 | bytes 1352708 | tf_op jit(solution)/shard_map/while/body/eval_jaxpr/reduce_sum | solution.py:29
  144.0 19.2 %fusion.6 = f32[12,88,256]{2,1,0:T(8,128)S(1)} fusion(f32[]{:T(128)} %bitcast.26, f32[64,12,88]{2,1,0:T(8,128)S(1)} %bitcast_convert_fusion.2, f32[256]{0:T(256)S(1)} %bitcast.34), kind=kLoop, calls=%fused_computation.2.clone.1 | loop fusion | flops 86237184 | bytes 1352708 | tf_op jit(solution)/shard_map/while/body/eval_jaxpr/reduce_sum | solution.py:29
  166.1 19.2 %fusion.6 = f32[12,88,256]{2,1,0:T(8,128)S(1)} fusion(f32[]{:T(128)} %bitcast.26, f32[64,12,88]{2,1,0:T(8,128)S(1)} %bitcast_convert_fusion.2, f32[256]{0:T(256)S(1)} %bitcast.34), kind=kLoop, calls=%fused_computation.2.clone.1 | loop fusion | flops 86237184 | bytes 1352708 | tf_op jit(solution)/shard_map/while/body/eval_jaxpr/reduce_sum | solution.py:29
  188.2 19.2 %fusion.6 = f32[12,88,256]{2,1,0:T(8,128)S(1)} fusion(f32[]{:T(128)} %bitcast.26, f32[64,12,88]{2,1,0:T(8,128)S(1)} %bitcast_convert_fusion.2, f32[256]{0:T(256)S(1)} %bitcast.34), kind=kLoop, calls=%fused_computation.2.clone.1 | loop fusion | flops 86237184 | bytes 1352708 | tf_op jit(solution)/shard_map/while/body/eval_jaxpr/reduce_sum | solution.py:29
  207.6 1.3 collective-permute-start
  208.9 1.3 collective-permute-start.1
  210.3 3.7 %collective-permute-done.1 = bf16[12,6,2,256]{3,2,1,0:T(2,128)(2,1)S(1)} collective-permute-done((bf16[12,6,2,256]{3,2,1,0:T(2,128)(2,1)S(1)}, bf16[12,6,2,256]{3,2,1,0:T(2,128)(2,1)S(1)}, u32[]{:S(2)}, u32[]{:S(2)}) %collective-permute-start.1) | collective-permute-done | bytes 73760 | tf_op jit(solution)/shard_map/ppermute | solution.py:19
  214.7 5.6 %collective-permute-start.2 = (bf16[2,6,92,256]{3,2,1,0:T(8,128)(2,1)S(1)}, bf16[2,6,92,256]{3,2,1,0:T(8,128)(2,1)S(1)}, u32[]{:S(2)}, u32[]{:S(2)}) collective-permute-start(bf16[2,6,92,256]{3,2,1,0:T(8,128)(2,1)S(1)} %get-tuple-element.81), channel_id=1, source_target_pairs={{0,1},{1,2},{2,3},{3,4},{4,5},{5,6},{6,7},{8,9},{9,10},{10,11},{11... | collective-permute-start | bytes 1695752 | tf_op jit(solution)/shard_map/ppermute | solution.py:17
  220.4 2.1 collective-permute-start.3
  222.5 4.7 %collective-permute-done.2 = bf16[2,6,92,256]{3,2,1,0:T(8,128)(2,1)S(1)} collective-permute-done((bf16[2,6,92,256]{3,2,1,0:T(8,128)(2,1)S(1)}, bf16[2,6,92,256]{3,2,1,0:T(8,128)(2,1)S(1)}, u32[]{:S(2)}, u32[]{:S(2)}) %collective-permute-start.2) | collective-permute-done | bytes 565280 | tf_op jit(solution)/shard_map/ppermute | solution.py:17
  227.2 8.0 %collective-permute-done.3 = bf16[2,6,92,256]{3,2,1,0:T(8,128)(2,1)S(1)} collective-permute-done((bf16[2,6,92,256]{3,2,1,0:T(8,128)(2,1)S(1)}, bf16[2,6,92,256]{3,2,1,0:T(8,128)(2,1)S(1)}, u32[]{:S(2)}, u32[]{:S(2)}) %collective-permute-start.3) | collective-permute-done | bytes 565280 | tf_op jit(solution)/shard_map/ppermute | solution.py:19
  235.1 4.4 %maximum_convert_fusion = f32[16,6,92,256]{3,2,1,0:T(8,128)} fusion(bf16[2,6,92,256]{3,2,1,0:T(8,128)(2,1)S(1)} %collective-permute-done.3, bf16[12,6,2,256]{3,2,1,0:T(2,128)(2,1)S(1)} %collective-permute-done.1, bf16[12,6,88,256]{3,2,1,0:T(8,128)(2,1)S(1)} %bitcast.32, bf16[12,6,2,256]{3,2,1,0:T(2,128)(2,1)S(1)} %collective-permute-done, ...), kind=kLoop, calls=%fused_computation.16 | loop fusion | flops 22609920 | bytes 13565952 | tf_op jit(solution)/shard_map/convert_element_type | solution.py:47
  239.6 13.6 %slice_add_fusion = f32[12,6,92,256]{3,2,1,0:T(8,128)S(1)} fusion(f32[16,6,92,256]{3,2,1,0:T(8,128)} %maximum_convert_fusion), kind=kLoop, calls=%fused_computation.6 | loop fusion | flops 6782976 | bytes 40697856 | tf_op jit(solution)/shard_map/add | solution.py:49
  253.2 4.2 %fusion.3 = bf16[12,6,88,256]{3,2,1,0:T(8,128)(2,1)} fusion(f32[12,6,92,256]{3,2,1,0:T(8,128)S(1)} %slice_add_fusion), kind=kLoop, calls=%fused_computation.12 | loop fusion | flops 9732096 | bytes 35684352 | tf_op jit(solution)/shard_map/convert_element_type | solution.py:62
  (32 shorter events, 16.1 us)
Async XLA Ops:
  25.2 25.7 %all-to-all-start = ((bf16[4,2,50688]{2,1,0:T(2,128)(2,1)}), bf16[4,2,50688]{2,1,0:T(2,128)(2,1)}, u32[]{:S(2)}, u32[]{:S(2)}) async-start(bf16[4,2,50688]{2,1,0:T(2,128)(2,1)} %reshape.26), calls=%async_computation | async-start | bytes 1622016 | tf_op jit(solution)/shard_map/all_to_all | solution.py:42
  61.3 13.5 %copy-start = (f32[6]{0:T(128)S(1)}, f32[6]{0:T(128)}, u32[]{:S(2)}) copy-start(f32[6]{0:T(128)} %param.9) | copy-start | bytes 76
  207.6 2.7 %collective-permute-start = (bf16[12,6,2,256]{3,2,1,0:T(2,128)(2,1)S(1)}, bf16[12,6,2,256]{3,2,1,0:T(2,128)(2,1)S(1)}, u32[]{:S(2)}, u32[]{:S(2)}) collective-permute-start(bf16[12,6,2,256]{3,2,1,0:T(2,128)(2,1)S(1)} %get-tuple-element.83), channel_id=1, source_target_pairs={{0,8},{8,16},{16,24},{1,9},{9,17},{17,25},{2,10},{10,18},{18,26},{... | collective-permute-start | bytes 221192 | tf_op jit(solution)/shard_map/ppermute | solution.py:17
  208.9 5.1 %collective-permute-start.1 = (bf16[12,6,2,256]{3,2,1,0:T(2,128)(2,1)S(1)}, bf16[12,6,2,256]{3,2,1,0:T(2,128)(2,1)S(1)}, u32[]{:S(2)}, u32[]{:S(2)}) collective-permute-start(bf16[12,6,2,256]{3,2,1,0:T(2,128)(2,1)S(1)} %get-tuple-element.84), channel_id=1, source_target_pairs={{8,0},{16,8},{24,16},{9,1},{17,9},{25,17},{10,2},{18,10},{26,18},{... | collective-permute-start | bytes 221192 | tf_op jit(solution)/shard_map/ppermute | solution.py:19
  214.7 12.4 %collective-permute-start.2 = (bf16[2,6,92,256]{3,2,1,0:T(8,128)(2,1)S(1)}, bf16[2,6,92,256]{3,2,1,0:T(8,128)(2,1)S(1)}, u32[]{:S(2)}, u32[]{:S(2)}) collective-permute-start(bf16[2,6,92,256]{3,2,1,0:T(8,128)(2,1)S(1)} %get-tuple-element.81), channel_id=1, source_target_pairs={{0,1},{1,2},{2,3},{3,4},{4,5},{5,6},{6,7},{8,9},{9,10},{10,11},{11... | collective-permute-start | bytes 1695752 | tf_op jit(solution)/shard_map/ppermute | solution.py:17
  220.4 14.8 %collective-permute-start.3 = (bf16[2,6,92,256]{3,2,1,0:T(8,128)(2,1)S(1)}, bf16[2,6,92,256]{3,2,1,0:T(8,128)(2,1)S(1)}, u32[]{:S(2)}, u32[]{:S(2)}) collective-permute-start(bf16[2,6,92,256]{3,2,1,0:T(8,128)(2,1)S(1)} %get-tuple-element.82), channel_id=1, source_target_pairs={{1,0},{2,1},{3,2},{4,3},{5,4},{6,5},{7,6},{9,8},{10,9},{11,10},{12... | collective-permute-start | bytes 1695752 | tf_op jit(solution)/shard_map/ppermute | solution.py:19
where the time goes:
time: 258 us; the launch traced here: 257 us
  other arithmetic  147 us (57%)
  local copies, waits for them, and re-layouts  54.4 us (21%)
  waiting for transfers between devices  36.7 us (14%)
  starting transfers between devices  15.7 us (6%)
  loops' own time  3.53 us (1%)
    reduce_sum x6, other arithmetic, var_density(): total = jnp.sum(jnp.exp(-0.5 * scaled * scaled), axis=0)  115 us
    all_to_all x1, waiting for transfers between devices, shards(): lax.all_to_all(values, 'member', split_axis=3, concat_axis=0, tiled=True)  20.2 us
    unnamed x5, local copies, waits for them, and re-layouts  19.7 us
    add x1, other arithmetic, shards(): padded[0:rows] + padded[1:rows + 1] + padded[2:rows + 2]  13.6 us
    all_to_all x1, local copies, waits for them, and re-layouts, shards(): lax.all_to_all(values, 'member', split_axis=3, concat_axis=0, tiled=True)  13.5 us
    convert_element_type x1, local copies, waits for them, and re-layouts, shards(): values = (codes.astype(jnp.float32) * scale[..., None]).astype(jnp.bfloat16)  13.3 us
    ppermute x2, waiting for transfers between devices, extended(): lax.ppermute(head, axis, [((i + 1) % count, i) for i in range(ends)])  11.7 us
    dynamic_slice x12, local copies, waits for them, and re-layouts, block_density(): lax.map(lambda t: var_density(t[0], t[1], t[2]), (items, centers, widths))  7.72 us
  transfers between devices with their start and end apart: 5, of which 5 were waited for; matrix products, arithmetic and copies ran while one was open for 0% of the time, Pallas kernels for 0%

commit v1 on v0

v1 whole, which is shorter than its diff:
```python
import functools
import math

import jax
import jax.numpy as jnp
import numpy as np
from jax import lax
from jax.experimental import pallas as pl
from jax.experimental.pallas import tpu as pltpu
from jax.sharding import PartitionSpec as P

REACH = 2
FINE = 256.0
OUTSIDE = 16.0
HALF = 384
POINTS = 2 * HALF
FIELDS = 16
WORDS = POINTS // FIELDS
VMEM = 48 * 1024 * 1024


def regroup_kernel(n, cells, width, codes_ref, scale_ref, out_ref):
    members, rows, items, _ = codes_ref.shape
    wide = cells + 2 * REACH
    edge = jnp.full((members, REACH), OUTSIDE, jnp.float32)
    rest = jnp.full((members, width - rows * wide), OUTSIDE, jnp.float32)
    for v in range(items):
        lines = []
        for r in range(rows):
            line = codes_ref[:, r, v, :].astype(jnp.float32)
            line = line * scale_ref[v, :, r : r + 1]
            lines.append(jnp.concatenate([edge, line, edge], axis=1))
        for d in range(n):
            parts = [line[:, d * cells : d * cells + wide] for line in lines]
            out_ref[d, v] = jnp.concatenate(parts + [rest], axis=1).astype(jnp.bfloat16)


def density_kernel(vals_ref, centers_ref, widths_ref, out_ref, table, words, steps, counts, bytes4):
    item = pl.program_id(0)
    n, _, members, width = vals_ref.shape
    total = n * members
    bins = centers_ref.shape[1]
    wide = widths_ref[item]

    point = lax.broadcasted_iota(jnp.int32, (1, POINTS), 1)
    mag = jnp.where(point >= HALF, point - HALF, point)
    octave = jnp.maximum(mag - 64, 0) >> 6
    mag = jnp.where(mag < 128, mag, (mag - 64 * octave) << octave).astype(jnp.float32)
    value = jnp.where(point >= HALF, -mag, mag) * (1.0 / FINE)
    scaled = (centers_ref[0] - value) / wide
    table[...] = jnp.exp(-0.5 * scaled * scaled).astype(jnp.bfloat16)

    for i in range(n):
        vals = vals_ref[i, 0].astype(jnp.float32) * FINE
        size = jnp.abs(vals).astype(jnp.int32)
        octave = jnp.zeros_like(size)
        for limit in (128, 256, 512, 1024):
            octave = octave + jnp.where(size >= limit, 1, 0)
        index = (size >> octave) + 64 * octave + jnp.where(vals < 0, HALF, 0)
        field = (index * (65536 // WORDS + 1)) >> 16
        there = size < 2048
        words[i * members : (i + 1) * members] = jnp.where(there, index - WORDS * field, WORDS)
        steps[i * members : (i + 1) * members] = jnp.left_shift(1, jnp.where(there, 2 * field, 0))

    norm = 1.0 / (total * wide * math.sqrt(2.0 * math.pi))
    lanes = 128
    groups = width // lanes
    counts[...] = jnp.zeros_like(counts)

    def finish(g):
        dens = jnp.dot(table[...], counts[...], preferred_element_type=jnp.float32)
        out_ref[0, :, pl.ds(pl.multiple_of(g * lanes, lanes), lanes)] = (dens * norm).astype(jnp.bfloat16)

    def group(g, _):
        finish(jnp.maximum(g - 1, 0))
        at = pl.ds(pl.multiple_of(g * lanes, lanes), lanes)
        row = lax.broadcasted_iota(jnp.int32, (WORDS, lanes), 0)
        for start in range(0, total, 15):
            stop = min(start + 15, total)
            raw = odd = None
            for first in range(start, stop, 3):
                pair = None
                for m in range(first, min(first + 3, stop)):
                    one = jnp.where(row == words[m : m + 1, at], steps[m : m + 1, at], 0)
                    pair = one if pair is None else pair + one
                high = lax.shift_right_logical(pair, 2) & 0x33333333
                raw = pair if raw is None else raw + pair
                odd = high if odd is None else odd + high
            even = raw - (odd << 2)
            for k, four in enumerate((even, odd)):
                low = four & 0x0F0F0F0F
                high = lax.shift_right_logical(four, 4) & 0x0F0F0F0F
                if start == 0:
                    bytes4[k] = low
                    bytes4[k + 2] = high
                else:
                    bytes4[k] += low
                    bytes4[k + 2] += high
        for f in range(FIELDS):
            part = lax.shift_right_logical(bytes4[f % 4], 8 * (f // 4))
            if f // 4 < 3:
                part = part & 0xFF
            counts[f * WORDS : (f + 1) * WORDS] = part.astype(jnp.float32).astype(jnp.bfloat16)
        return 0

    lax.fori_loop(0, groups, group, 0)
    finish(groups - 1)


def window_kernel(rows, cells, own_ref, top_ref, bottom_ref, mix_ref, mix_top_ref, mix_bottom_ref, out_ref):
    edge = mix_top_ref.shape[0]
    dims = (((1,), (1,)), ((), ()))
    def mixed(mix, dens):
        return lax.dot_general(mix, dens, dims, preferred_element_type=jnp.float32)
    above = mixed(mix_top_ref[...], top_ref[0])
    below = mixed(mix_bottom_ref[...], bottom_ref[0])
    full = mixed(mix_ref[...], own_ref[0])
    for r in range(rows):
        part = full[r * cells : (r + 1) * cells]
        if r < REACH:
            part = part + above[r * cells : (r + 1) * cells]
        if r >= rows - REACH:
            at = edge - (rows - r) * cells
            part = part + below[at : at + cells]
        out_ref[r, 0] = (part / 25.0).astype(jnp.bfloat16)


def window(rows, first, cells, width, source, source_first):
    wide = cells + 2 * REACH
    out = np.arange(rows * cells)
    lane = np.arange(width)
    dr = np.abs((out // cells + first)[:, None] - (lane // wide + source_first)[None, :])
    dl = (lane % wide)[None, :] - (out % cells)[:, None]
    inside = (dr <= REACH) & (dl >= 0) & (dl <= 2 * REACH) & (lane < source * wide)[None, :]
    return jnp.asarray(inside, jnp.bfloat16)


def solution(mesh):
    n = mesh.shape["member"]
    count = mesh.shape["band"]

    def shards(codes, exponents, centers, widths):
        members, rows, items, lon = codes.shape
        bins = centers.shape[1]
        cells = lon // n
        wide = cells + 2 * REACH
        width = -(-rows * wide // 128) * 128
        scale = jnp.left_shift(1, exponents + 8).astype(jnp.float32) * (1.0 / FINE)
        scale = jnp.transpose(scale, (2, 0, 1))
        params = pltpu.CompilerParams(vmem_limit_bytes=VMEM)
        values = pl.pallas_call(
            functools.partial(regroup_kernel, n, cells, width),
            out_shape=jax.ShapeDtypeStruct((n, items, members, width), jnp.bfloat16),
            compiler_params=params,
        )(codes, scale)
        values = lax.all_to_all(values, "member", split_axis=0, concat_axis=0, tiled=True)
        dens = pl.pallas_call(
            density_kernel,
            grid=(items,),
            in_specs=[
                pl.BlockSpec((n, 1, members, width), lambda v: (0, v, 0, 0)),
                pl.BlockSpec((1, bins, 1), lambda v: (v, 0, 0)),
                pl.BlockSpec(memory_space=pltpu.SMEM),
            ],
            out_specs=pl.BlockSpec((1, bins, width), lambda v: (v, 0, 0)),
            out_shape=jax.ShapeDtypeStruct((items, bins, width), jnp.bfloat16),
            scratch_shapes=[
                pltpu.VMEM((bins, POINTS), jnp.bfloat16),
                pltpu.VMEM((n * members, width), jnp.int32),
                pltpu.VMEM((n * members, width), jnp.int32),
                pltpu.VMEM((POINTS, 128), jnp.bfloat16),
                pltpu.VMEM((4, WORDS, 128), jnp.int32),
            ],
            compiler_params=params,
        )(values, centers[:, :, None], widths)
        edge = REACH * wide
        head = dens[:, :, :edge]
        tail = dens[:, :, (rows - REACH) * wide : rows * wide]
        top = lax.ppermute(tail, "band", [(i, i + 1) for i in range(count - 1)])
        bottom = lax.ppermute(head, "band", [(i + 1, i) for i in range(count - 1)])
        mix = window(rows, 0, cells, width, rows, 0)
        mix_top = window(REACH, 0, cells, edge, REACH, -REACH)
        mix_bottom = window(REACH, rows - REACH, cells, edge, REACH, rows)
        whole = pl.BlockSpec(memory_space=pltpu.VMEM)
        return pl.pallas_call(
            functools.partial(window_kernel, rows, cells),
            grid=(items,),
            in_specs=[
                pl.BlockSpec((1, bins, width), lambda v: (v, 0, 0)),
                pl.BlockSpec((1, bins, edge), lambda v: (v, 0, 0)),
                pl.BlockSpec((1, bins, edge), lambda v: (v, 0, 0)),
                whole,
                whole,
                whole,
            ],
            out_specs=pl.BlockSpec((rows, 1, cells, bins), lambda v: (0, v, 0, 0)),
            out_shape=jax.ShapeDtypeStruct((rows, items, cells, bins), jnp.bfloat16),
            compiler_params=params,
        )(dens, top, bottom, mix, mix_top, mix_bottom)

    return jax.shard_map(
        shards,
        mesh=mesh,
        in_specs=(P("member", "band", None, None), P("member", "band", None), P(), P()),
        out_specs=P("band", None, "member", None),
        check_vma=False,
    )
```

time: 258 us -> 104 us (0.40)
  other arithmetic: 147 us -> 0.81 us
  Pallas kernels: 0 us -> 40.6 us
  local copies, waits for them, and re-layouts: 54.4 us -> 21 us
  waiting for transfers between devices: 36.7 us -> 28.7 us
  starting transfers between devices: 15.7 us -> 11.8 us
  loops' own time: 3.53 us -> 0 us
    reduce_sum x6 -> x0, other arithmetic: 115 us -> none  [var_density(): total = jnp.sum(jnp.exp(-0.5 * scaled * scaled), axis=0)]
    pallas_call x0 -> x3, Pallas kernels: none -> 40.6 us  [the longest x1 25.8 us: shards(): pl.pallas_call(density_kernel, grid=(items,), in_specs=[pl.BlockSpec((n,...]
    convert_element_type x9 -> x0, other arithmetic: 16.2 us -> none  [the longest x6 5.91 us: var_density(): field = item.astype(jnp.float32)]
    add x1 -> x0, other arithmetic: 13.6 us -> none  [shards(): padded[0:rows] + padded[1:rows + 1] + padded[2:rows + 2]]
    all_to_all x1 -> x0, local copies, waits for them, and re-layouts: 13.5 us -> none  [shards(): lax.all_to_all(values, 'member', split_axis=3, concat_axis=0, tiled=True)]
    convert_element_type x1 -> x0, local copies, waits for them, and re-layouts: 13.3 us -> none  [shards(): values = (codes.astype(jnp.float32) * scale[..., None]).astype(jnp.bfloat16)]
    unnamed x5 -> x21, local copies, waits for them, and re-layouts: 19.7 us -> 9.91 us
    ppermute x4 -> x2, waiting for transfers between devices: 16.5 us -> 8.22 us  [the longest x1 5.5 us: shards(): bottom = lax.ppermute(head, 'band', [(i + 1, i) for i in range(count - 1)])]
  transfers between devices with their start and end apart: 5 -> 3, of which waited for: 5 -> 3; matrix products, arithmetic and copies ran while one was open for 0% -> 5% of each run, Pallas kernels for 0% -> 0%
where the time goes in v1:
time: 104 us; the launch traced here: 103 us
  Pallas kernels  40.6 us (39%)
  waiting for transfers between devices  28.7 us (28%)
  local copies, waits for them, and re-layouts  21 us (20%)
  starting transfers between devices  11.8 us (11%)
    pallas_call x1, Pallas kernels, shards(): pl.pallas_call(density_kernel, grid=(items,), in_specs=[pl.BlockSpec((n,...  25.8 us
    all_to_all x1, waiting for transfers between devices, shards(): lax.all_to_all(values, 'member', split_axis=0, concat_axis=0, tiled=True)  20.5 us
    unnamed x21, local copies, waits for them, and re-layouts  9.91 us
    pallas_call x1, Pallas kernels, shards(): pl.pallas_call(functools.partial(window_kernel, rows, cells), grid=(items...  8.49 us
    pallas_call x1, Pallas kernels, shards(): pl.pallas_call(functools.partial(regroup_kernel, n, cells, width), out_sh...  6.34 us
    ppermute x1, waiting for transfers between devices, shards(): bottom = lax.ppermute(head, 'band', [(i + 1, i) for i in range(count - 1)])  5.5 us
    all_to_all x1, starting transfers between devices, shards(): lax.all_to_all(values, 'member', split_axis=0, concat_axis=0, tiled=True)  5.42 us
    ppermute x1, starting transfers between devices, shards(): top = lax.ppermute(tail, 'band', [(i, i + 1) for i in range(count - 1)])  4.44 us
  transfers between devices with their start and end apart: 3, of which 3 were waited for; matrix products, arithmetic and copies ran while one was open for 5% of the time, Pallas kernels for 0%

profile of v1, /device:TPU:1, one launch (start us, length us, event | category | flops | bytes accessed | tf_op | source)
XLA Modules:
  0.0 103.0 jit_solution(4369737731418359599)
XLA Ops:
  0.0 0.8 multiply_bitcast_fusion.scale_ref
  0.8 2.1 %copy.11.codes_ref = s32[16,12,6,352]{3,2,1,0:T(8,128)S(1)} copy(s32[16,12,6,352]{3,0,2,1:T(8,128)} %param.7) | data formatting | bytes 3244032 | tf_op args[0]
  2.9 6.3 %shard_map.73 = bf16[4,6,16,1152]{3,2,1,0:T(8,128)(2,1)} custom-call(s32[16,12,6,352]{3,2,1,0:T(8,128)S(1)} %copy.11.codes_ref, f32[6,16,12]{2,1,0:T(8,128)S(1)} %multiply_bitcast_fusion.scale_ref), custom_call_target="tpu_custom_call" | custom-call | tf_op jit(solution)/shard_map/pallas_call | solution.py:151
  9.3 5.4 %all-to-all-start = ((bf16[4,6,16,1152]{3,2,1,0:T(8,128)(2,1)}), bf16[4,6,16,1152]{3,2,1,0:T(8,128)(2,1)S(1)}, u32[]{:S(2)}, u32[]{:S(2)}) async-start(bf16[4,6,16,1152]{3,2,1,0:T(8,128)(2,1)} %shard_map.73), calls=%async_computation | async-start | bytes 1769472 | tf_op jit(solution)/shard_map/all_to_all | solution.py:156
  14.7 1.2 %copy.12.centers_ref = f32[6,256,1]{2,1,0:T(8,128)} copy(f32[6,256,1]{1,0,2:T(8,128)S(1)} %bitcast.3) | data formatting | bytes 12288 | tf_op jit(solution)/shard_map/broadcast_in_dim | solution.py:175
  15.9 20.5 %all-to-all-done.vals_ref = bf16[4,6,16,1152]{3,2,1,0:T(8,128)(2,1)S(1)} async-done(((bf16[4,6,16,1152]{3,2,1,0:T(8,128)(2,1)}), bf16[4,6,16,1152]{3,2,1,0:T(8,128)(2,1)S(1)}, u32[]{:S(2)}, u32[]{:S(2)}) %all-to-all-start) | async-done | bytes 884768 | tf_op jit(solution)/shard_map/all_to_all | solution.py:156
  36.4 0.9 copy-done.1
  37.3 1.2 %copy-done.2 = bf16[4,6,16,1152]{3,2,1,0:T(8,128)(2,1)S(1)} copy-done((bf16[4,6,16,1152]{3,2,1,0:T(8,128)(2,1)S(1)}, bf16[4,6,16,1152]{3,2,1,0:T(8,128)(2,1)}, u32[]{:S(2)}) %copy-start.2) | copy-done | bytes 884760
  38.5 1.1 %copy-done.4 = f32[6,256,1]{2,1,0:T(8,128)S(1)} copy-done((f32[6,256,1]{2,1,0:T(8,128)S(1)}, f32[6,256,1]{2,1,0:T(8,128)}, u32[]{:S(2)}) %copy-start.4) | copy-done | bytes 6168
  39.6 25.8 %shard_map.74.own_ref = bf16[6,256,1152]{2,1,0:T(8,128)(2,1)S(1)} custom-call(bf16[4,6,16,1152]{3,2,1,0:T(8,128)(2,1)S(1)} %copy-done.2, f32[6,256,1]{2,1,0:T(8,128)S(1)} %copy-done.4, f32[6]{0:T(128)S(1)} %copy-done.8), custom_call_target="tpu_custom_call" | custom-call | tf_op jit(solution)/shard_map/pallas_call | solution.py:157
  65.5 1.9 %fusion = (bf16[6,256,184]{2,1,0:T(8,128)(2,1)}, bf16[6,256,184]{2,1,0:T(8,128)(2,1)}) fusion(bf16[6,256,1152]{2,1,0:T(8,128)(2,1)S(1)} %shard_map.74.own_ref), kind=kLoop, calls=%fused_computation.1 | loop fusion | bytes 2260992 | tf_op jit(solution)/shard_map/slice | solution.py:177
  67.3 2.2 %copy.13 = bf16[6,256,184]{1,2,0:T(8,128)(2,1)} copy(bf16[6,256,184]{2,1,0:T(8,128)(2,1)} %get-tuple-element.6) | data formatting | bytes 1130496 | tf_op jit(solution)/shard_map/slice | solution.py:178
  69.6 4.4 %collective-permute-start = (bf16[6,256,184]{1,2,0:T(8,128)(2,1)}, bf16[6,256,184]{1,2,0:T(8,128)(2,1)}, u32[]{:S(2)}, u32[]{:S(2)}) collective-permute-start(bf16[6,256,184]{1,2,0:T(8,128)(2,1)} %copy.13), channel_id=1, source_target_pairs={{0,1},{1,2},{2,3},{3,4},{4,5},{5,6},{6,7},{8,9},{9,10},{10,11},{11... | collective-permute-start | bytes 1695752 | tf_op jit(solution)/shard_map/ppermute | solution.py:179
  74.0 2.2 %copy.14 = bf16[6,256,184]{1,2,0:T(8,128)(2,1)} copy(bf16[6,256,184]{2,1,0:T(8,128)(2,1)} %get-tuple-element.5) | data formatting | bytes 1130496 | tf_op jit(solution)/shard_map/slice | solution.py:177
  76.2 1.9 %collective-permute-start.1 = (bf16[6,256,184]{1,2,0:T(8,128)(2,1)}, bf16[6,256,184]{1,2,0:T(8,128)(2,1)}, u32[]{:S(2)}, u32[]{:S(2)}) collective-permute-start(bf16[6,256,184]{1,2,0:T(8,128)(2,1)} %copy.14), channel_id=1, source_target_pairs={{1,0},{2,1},{3,2},{4,3},{5,4},{6,5},{7,6},{9,8},{10,9},{11,10},{12... | collective-permute-start | bytes 1695752 | tf_op jit(solution)/shard_map/ppermute | solution.py:180
  78.1 2.7 %collective-permute-done = bf16[6,256,184]{1,2,0:T(8,128)(2,1)} collective-permute-done((bf16[6,256,184]{1,2,0:T(8,128)(2,1)}, bf16[6,256,184]{1,2,0:T(8,128)(2,1)}, u32[]{:S(2)}, u32[]{:S(2)}) %collective-permute-start) | collective-permute-done | bytes 565280 | tf_op jit(solution)/shard_map/ppermute | solution.py:179
  80.9 2.2 %copy.15.top_ref = bf16[6,256,184]{2,1,0:T(8,128)(2,1)} copy(bf16[6,256,184]{1,2,0:T(8,128)(2,1)} %collective-permute-done) | data formatting | bytes 1130496 | tf_op jit(solution)/shard_map/ppermute | solution.py:179
  83.1 5.5 %collective-permute-done.1 = bf16[6,256,184]{1,2,0:T(8,128)(2,1)} collective-permute-done((bf16[6,256,184]{1,2,0:T(8,128)(2,1)}, bf16[6,256,184]{1,2,0:T(8,128)(2,1)}, u32[]{:S(2)}, u32[]{:S(2)}) %collective-permute-start.1) | collective-permute-done | bytes 565280 | tf_op jit(solution)/shard_map/ppermute | solution.py:180
  88.6 1.3 %copy.16.bottom_ref = bf16[6,256,184]{2,1,0:T(8,128)(2,1)S(1)} copy(bf16[6,256,184]{1,2,0:T(8,128)(2,1)} %collective-permute-done.1) | data formatting | bytes 1130496 | tf_op jit(solution)/shard_map/ppermute | solution.py:180
  89.9 1.1 %copy-done.3 = bf16[6,256,184]{2,1,0:T(8,128)(2,1)S(1)} copy-done((bf16[6,256,184]{2,1,0:T(8,128)(2,1)S(1)}, bf16[6,256,184]{2,1,0:T(8,128)(2,1)}, u32[]{:S(2)}) %copy-start.3) | copy-done | bytes 565272
  91.0 1.7 %copy-done.5 = bf16[1056,1152]{1,0:T(8,128)(2,1)S(1)} copy-done((bf16[1056,1152]{1,0:T(8,128)(2,1)S(1)}, bf16[1056,1152]{1,0:T(8,128)(2,1)}, u32[]{:S(2)}) %copy-start.5) | copy-done | bytes 2433048
  92.7 0.9 copy-done.6
  93.6 0.9 copy-done.7
  94.5 8.5 %shard_map.75 = bf16[12,6,88,256]{3,2,1,0:T(8,128)(2,1)} custom-call(bf16[6,256,1152]{2,1,0:T(8,128)(2,1)} %copy-done, bf16[6,256,184]{2,1,0:T(8,128)(2,1)S(1)} %copy-done.3, bf16[6,256,184]{2,1,0:T(8,128)(2,1)S(1)} %copy.16.bottom_ref, bf16[1056,1152]{1,0:T(8,128)(2,1)S(1)} %copy-done.5, bf16[176,184]{1,0:T(8,128)(2,1)S(1)} %copy-done.7, ...), custom_call_target="tpu_custom_call" | custom-call | tf_op jit(solution)/shard_map/pallas_call | solution.py:185
  (13 shorter events, 0.0 us)
Async XLA Ops:
  2.9 11.8 %copy-start.9 = (f32[6,256]{1,0:T(8,128)S(1)}, f32[6,256]{1,0:T(8,128)}, u32[]{:S(2)}) copy-start(f32[6,256]{1,0:T(8,128)} %param.9) | copy-start | bytes 18436
  2.9 34.4 %copy-start.8 = (f32[6]{0:T(128)S(1)}, f32[6]{0:T(128)}, u32[]{:S(2)}) copy-start(f32[6]{0:T(128)} %widths_ref.1) | copy-start | bytes 76
  9.3 27.1 %all-to-all-start = ((bf16[4,6,16,1152]{3,2,1,0:T(8,128)(2,1)}), bf16[4,6,16,1152]{3,2,1,0:T(8,128)(2,1)S(1)}, u32[]{:S(2)}, u32[]{:S(2)}) async-start(bf16[4,6,16,1152]{3,2,1,0:T(8,128)(2,1)} %shard_map.73), calls=%async_computation | async-start | bytes 1769472 | tf_op jit(solution)/shard_map/all_to_all | solution.py:156
  36.4 0.9 copy-start.1
  37.3 1.2 %copy-start.2 = (bf16[4,6,16,1152]{3,2,1,0:T(8,128)(2,1)S(1)}, bf16[4,6,16,1152]{3,2,1,0:T(8,128)(2,1)}, u32[]{:S(2)}) copy-start(bf16[4,6,16,1152]{3,2,1,0:T(8,128)(2,1)} %copy-done.1) | copy-start | bytes 2654212
  38.5 1.1 %copy-start.4 = (f32[6,256,1]{2,1,0:T(8,128)S(1)}, f32[6,256,1]{2,1,0:T(8,128)}, u32[]{:S(2)}) copy-start(f32[6,256,1]{2,1,0:T(8,128)} %copy.12.centers_ref) | copy-start | bytes 18436
  65.5 17.6 %copy-start = (bf16[6,256,1152]{2,1,0:T(8,128)(2,1)}, bf16[6,256,1152]{2,1,0:T(8,128)(2,1)S(1)}, u32[]{:S(2)}) copy-start(bf16[6,256,1152]{2,1,0:T(8,128)(2,1)S(1)} %shard_map.74.own_ref) | copy-start | bytes 10616836
  69.6 11.3 %collective-permute-start = (bf16[6,256,184]{1,2,0:T(8,128)(2,1)}, bf16[6,256,184]{1,2,0:T(8,128)(2,1)}, u32[]{:S(2)}, u32[]{:S(2)}) collective-permute-start(bf16[6,256,184]{1,2,0:T(8,128)(2,1)} %copy.13), channel_id=1, source_target_pairs={{0,1},{1,2},{2,3},{3,4},{4,5},{5,6},{6,7},{8,9},{9,10},{10,11},{11... | collective-permute-start | bytes 1695752 | tf_op jit(solution)/shard_map/ppermute | solution.py:179
  76.2 12.3 %collective-permute-start.1 = (bf16[6,256,184]{1,2,0:T(8,128)(2,1)}, bf16[6,256,184]{1,2,0:T(8,128)(2,1)}, u32[]{:S(2)}, u32[]{:S(2)}) collective-permute-start(bf16[6,256,184]{1,2,0:T(8,128)(2,1)} %copy.14), channel_id=1, source_target_pairs={{1,0},{2,1},{3,2},{4,3},{5,4},{6,5},{7,6},{9,8},{10,9},{11,10},{12... | collective-permute-start | bytes 1695752 | tf_op jit(solution)/shard_map/ppermute | solution.py:180
  89.9 1.1 %copy-start.3 = (bf16[6,256,184]{2,1,0:T(8,128)(2,1)S(1)}, bf16[6,256,184]{2,1,0:T(8,128)(2,1)}, u32[]{:S(2)}) copy-start(bf16[6,256,184]{2,1,0:T(8,128)(2,1)} %copy.15.top_ref) | copy-start | bytes 1695748
  91.0 1.7 %copy-start.5 = (bf16[1056,1152]{1,0:T(8,128)(2,1)S(1)}, bf16[1056,1152]{1,0:T(8,128)(2,1)}, u32[]{:S(2)}) copy-start(bf16[1056,1152]{1,0:T(8,128)(2,1)} %constant.12.clone.mix_ref) | copy-start | bytes 7299076
  92.7 0.9 copy-start.6
  93.6 0.9 copy-start.7

commit v2 on v1

v2 whole, which is shorter than its diff:
```python
import functools
import math

import jax
import jax.numpy as jnp
import numpy as np
from jax import lax
from jax.experimental import pallas as pl
from jax.experimental.pallas import tpu as pltpu
from jax.sharding import PartitionSpec as P

MESH = pl.DeviceIdType.MESH
REACH = 2
FINE = 256.0
OUTSIDE = 16.0
HALF = 384
POINTS = 2 * HALF
FIELDS = 16
WORDS = POINTS // FIELDS
VMEM = 48 * 1024 * 1024


def regroup(codes_ref, scale_ref, v, n, cells, width):
    rows, _, members, _ = codes_ref.shape
    wide = cells + 2 * REACH
    edge = jnp.full((members, REACH), OUTSIDE, jnp.float32)
    rest = jnp.full((members, width - rows * wide), OUTSIDE, jnp.float32)
    lines = []
    for r in range(rows):
        line = codes_ref[r, v].astype(jnp.float32)
        line = line * scale_ref[v, :, r : r + 1]
        lines.append(jnp.concatenate([edge, line, edge], axis=1))
    for d in range(n):
        parts = [line[:, d * cells : d * cells + wide] for line in lines]
        yield d, jnp.concatenate(parts + [rest], axis=1).astype(jnp.bfloat16)


def density_kernel(
    n, count, cells, width, lead, trail,
    codes_ref, scale_ref, centers_ref, widths_ref,
    own_ref, top_ref, bottom_ref,
    send, recv, dens, zeros, table, words, steps, counts, bytes4,
    send_sem, recv_sem, up_sem, down_sem, own_sem, zero_sem,
):
    rows, items, members, _ = codes_ref.shape
    total = n * members
    bins = centers_ref.shape[1]
    lanes = 128
    groups = width // lanes
    me = lax.axis_index("member")
    band = lax.axis_index("band")

    barrier = pltpu.get_barrier_semaphore()
    for o in range(1, n):
        pl.semaphore_signal(barrier, inc=1, device_id=(lax.rem(me + o, n), band), device_id_type=MESH)

    @pl.when(band > 0)
    def _():
        pl.semaphore_signal(barrier, inc=1, device_id=(me, band - 1), device_id_type=MESH)

    @pl.when(band < count - 1)
    def _():
        pl.semaphore_signal(barrier, inc=1, device_id=(me, band + 1), device_id_type=MESH)

    def outgoing(v, o):
        return pltpu.make_async_remote_copy(
            src_ref=send.at[v, lax.rem(me + o, n)],
            dst_ref=recv.at[v, o - 1],
            send_sem=send_sem.at[v, o - 1],
            recv_sem=recv_sem.at[v, o - 1],
            device_id=(lax.rem(me + o, n), band),
            device_id_type=MESH,
        )

    def upward(v):
        return pltpu.make_async_remote_copy(
            src_ref=dens.at[v, :, pl.ds(width - trail, trail)],
            dst_ref=top_ref.at[v],
            send_sem=up_sem.at[v, 0],
            recv_sem=up_sem.at[v, 1],
            device_id=(me, band + 1),
            device_id_type=MESH,
        )

    def downward(v):
        return pltpu.make_async_remote_copy(
            src_ref=dens.at[v, :, pl.ds(0, lead)],
            dst_ref=bottom_ref.at[v],
            send_sem=down_sem.at[v, 0],
            recv_sem=down_sem.at[v, 1],
            device_id=(me, band - 1),
            device_id_type=MESH,
        )

    def blank(v, side):
        if side == 0:
            return pltpu.make_async_copy(zeros.at[:, pl.ds(0, trail)], top_ref.at[v], zero_sem.at[0, v])
        return pltpu.make_async_copy(zeros.at[:, pl.ds(0, lead)], bottom_ref.at[v], zero_sem.at[1, v])

    def keep(v):
        return pltpu.make_async_copy(dens.at[v], own_ref.at[v], own_sem.at[v])

    for v in range(items):
        for d, block in regroup(codes_ref, scale_ref, v, n, cells, width):
            send[v, d] = block
        if v == 0:
            beside = jnp.where(band > 0, 1, 0) + jnp.where(band < count - 1, 1, 0)
            pl.semaphore_wait(barrier, n - 1 + beside)
        for o in range(1, n):
            outgoing(v, o).start()

    zeros[...] = jnp.zeros_like(zeros)

    @pl.when(band == 0)
    def _():
        for v in range(items):
            blank(v, 0).start()

    @pl.when(band == count - 1)
    def _():
        for v in range(items):
            blank(v, 1).start()

    counts[...] = jnp.zeros_like(counts)

    def item(v, _):
        wide = widths_ref[v]
        point = lax.broadcasted_iota(jnp.int32, (1, POINTS), 1)
        mag = jnp.where(point >= HALF, point - HALF, point)
        octave = jnp.maximum(mag - 64, 0) >> 6
        mag = jnp.where(mag < 128, mag, (mag - 64 * octave) << octave).astype(jnp.float32)
        value = jnp.where(point >= HALF, -mag, mag) * (1.0 / FINE)
        cross = lax.broadcasted_iota(jnp.int32, (bins, bins), 0) == lax.broadcasted_iota(jnp.int32, (bins, bins), 1)
        center = jnp.sum(jnp.where(cross, centers_ref[pl.ds(v, 1), :], 0.0), axis=1, keepdims=True)
        scaled = (center - value) / wide
        table[...] = jnp.exp(-0.5 * scaled * scaled).astype(jnp.bfloat16)

        for i in range(n):
            if i == 0:
                vals = send[v, me]
            else:
                outgoing(v, i).wait_recv()
                vals = recv[v, i - 1]
            vals = vals.astype(jnp.float32) * FINE
            size = jnp.abs(vals).astype(jnp.int32)
            octave = jnp.zeros_like(size)
            for limit in (128, 256, 512, 1024):
                octave = octave + jnp.where(size >= limit, 1, 0)
            index = (size >> octave) + 64 * octave + jnp.where(vals < 0, HALF, 0)
            field = (index * (65536 // WORDS + 1)) >> 16
            there = size < 2048
            words[i * members : (i + 1) * members] = jnp.where(there, index - WORDS * field, WORDS)
            steps[i * members : (i + 1) * members] = jnp.left_shift(1, jnp.where(there, 2 * field, 0))

        norm = 1.0 / (total * wide * math.sqrt(2.0 * math.pi))

        def finish(g):
            part = jnp.dot(table[...], counts[...], preferred_element_type=jnp.float32)
            at = pl.ds(pl.multiple_of(g * lanes, lanes), lanes)
            dens[v, :, at] = (part * norm).astype(jnp.bfloat16)

        def group(g, _):
            finish(jnp.maximum(g - 1, 0))
            at = pl.ds(pl.multiple_of(g * lanes, lanes), lanes)
            row = lax.broadcasted_iota(jnp.int32, (WORDS, lanes), 0)
            for start in range(0, total, 15):
                stop = min(start + 15, total)
                raw = odd = None
                for first in range(start, stop, 3):
                    pair = None
                    for m in range(first, min(first + 3, stop)):
                        one = jnp.where(row == words[m : m + 1, at], steps[m : m + 1, at], 0)
                        pair = one if pair is None else pair + one
                    high = lax.shift_right_logical(pair, 2) & 0x33333333
                    raw = pair if raw is None else raw + pair
                    odd = high if odd is None else odd + high
                even = raw - (odd << 2)
                for k, four in enumerate((even, odd)):
                    low = four & 0x0F0F0F0F
                    high = lax.shift_right_logical(four, 4) & 0x0F0F0F0F
                    if start == 0:
                        bytes4[k] = low
                        bytes4[k + 2] = high
                    else:
                        bytes4[k] += low
                        bytes4[k + 2] += high
            for f in range(FIELDS):
                part = lax.shift_right_logical(bytes4[f % 4], 8 * (f // 4))
                if f // 4 < 3:
                    part = part & 0xFF
                counts[f * WORDS : (f + 1) * WORDS] = part.astype(jnp.float32).astype(jnp.bfloat16)
            return 0

        lax.fori_loop(0, groups, group, 0)
        finish(groups - 1)
        keep(v).start()

        @pl.when(band > 0)
        def _():
            downward(v).start()

        @pl.when(band < count - 1)
        def _():
            upward(v).start()

        return 0

    lax.fori_loop(0, items, item, 0)

    for v in range(items):
        keep(v).wait()
        for o in range(1, n):
            outgoing(v, o).wait_send()

    @pl.when(band > 0)
    def _():
        for v in range(items):
            downward(v).wait_send()
            upward(v).wait_recv()

    @pl.when(band < count - 1)
    def _():
        for v in range(items):
            upward(v).wait_send()
            downward(v).wait_recv()

    @pl.when(band == 0)
    def _():
        for v in range(items):
            blank(v, 0).wait()

    @pl.when(band == count - 1)
    def _():
        for v in range(items):
            blank(v, 1).wait()


def window_kernel(rows, cells, own_ref, top_ref, bottom_ref, mix_ref, mix_top_ref, mix_bottom_ref, out_ref):
    edge = mix_top_ref.shape[0]
    dims = (((1,), (1,)), ((), ()))
    def mixed(mix, dens):
        return lax.dot_general(mix, dens, dims, preferred_element_type=jnp.float32)
    above = mixed(mix_top_ref[...], top_ref[0])
    below = mixed(mix_bottom_ref[...], bottom_ref[0])
    full = mixed(mix_ref[...], own_ref[0])
    for r in range(rows):
        part = full[r * cells : (r + 1) * cells]
        if r < REACH:
            part = part + above[r * cells : (r + 1) * cells]
        if r >= rows - REACH:
            at = edge - (rows - r) * cells
            part = part + below[at : at + cells]
        out_ref[r, 0] = (part / 25.0).astype(jnp.bfloat16)


def window(rows, first, cells, lanes, source_rows, source_first):
    wide = cells + 2 * REACH
    out = np.arange(rows * cells)
    row, place = lanes // wide, lanes % wide
    dr = np.abs((out // cells + first)[:, None] - (row + source_first)[None, :])
    dl = place[None, :] - (out % cells)[:, None]
    real = (row >= source_rows[0]) & (row < source_rows[1])
    inside = (dr <= REACH) & (dl >= 0) & (dl <= 2 * REACH) & real[None, :]
    return jnp.asarray(inside, jnp.bfloat16)


def solution(mesh):
    n = mesh.shape["member"]
    count = mesh.shape["band"]

    def shards(codes, exponents, centers, widths):
        members, rows, items, lon = codes.shape
        bins = centers.shape[1]
        cells = lon // n
        wide = cells + 2 * REACH
        width = -(-rows * wide // 128) * 128
        scale = jnp.left_shift(1, exponents + 8).astype(jnp.float32) * (1.0 / FINE)
        scale = jnp.transpose(scale, (2, 0, 1))
        codes = jnp.transpose(codes, (1, 2, 0, 3))
        lead = -(-REACH * wide // 128) * 128
        trail = width - (rows - REACH) * wide // 128 * 128
        params = pltpu.CompilerParams(vmem_limit_bytes=VMEM)
        vmem = pl.BlockSpec(memory_space=pltpu.VMEM)
        hbm = pl.BlockSpec(memory_space=pl.ANY)
        dens, top, bottom = pl.pallas_call(
            functools.partial(density_kernel, n, count, cells, width, lead, trail),
            in_specs=[vmem, vmem, vmem, pl.BlockSpec(memory_space=pltpu.SMEM)],
            out_specs=[hbm, hbm, hbm],
            out_shape=[
                jax.ShapeDtypeStruct((items, bins, width), jnp.bfloat16),
                jax.ShapeDtypeStruct((items, bins, trail), jnp.bfloat16),
                jax.ShapeDtypeStruct((items, bins, lead), jnp.bfloat16),
            ],
            scratch_shapes=[
                pltpu.VMEM((items, n, members, width), jnp.bfloat16),
                pltpu.VMEM((items, max(n - 1, 1), members, width), jnp.bfloat16),
                pltpu.VMEM((items, bins, width), jnp.bfloat16),
                pltpu.VMEM((bins, max(lead, trail)), jnp.bfloat16),
                pltpu.VMEM((bins, POINTS), jnp.bfloat16),
                pltpu.VMEM((n * members, width), jnp.int32),
                pltpu.VMEM((n * members, width), jnp.int32),
                pltpu.VMEM((POINTS, 128), jnp.bfloat16),
                pltpu.VMEM((4, WORDS, 128), jnp.int32),
                pltpu.SemaphoreType.DMA((items, n)),
                pltpu.SemaphoreType.DMA((items, n)),
                pltpu.SemaphoreType.DMA((items, 2)),
                pltpu.SemaphoreType.DMA((items, 2)),
                pltpu.SemaphoreType.DMA((items,)),
                pltpu.SemaphoreType.DMA((2, items)),
            ],
            compiler_params=pltpu.CompilerParams(
                vmem_limit_bytes=VMEM, collective_id=0, has_side_effects=True
            ),
        )(codes, scale, centers, widths)
        mix = window(rows, 0, cells, np.arange(width), (0, rows), 0)
        mix_top = window(REACH, 0, cells, np.arange(width - trail, width), (rows - REACH, rows), -rows)
        mix_bottom = window(REACH, rows - REACH, cells, np.arange(lead), (0, REACH), rows)
        whole = pl.BlockSpec(memory_space=pltpu.VMEM)
        return pl.pallas_call(
            functools.partial(window_kernel, rows, cells),
            grid=(items,),
            in_specs=[
                pl.BlockSpec((1, bins, width), lambda v: (v, 0, 0)),
                pl.BlockSpec((1, bins, trail), lambda v: (v, 0, 0)),
                pl.BlockSpec((1, bins, lead), lambda v: (v, 0, 0)),
                whole,
                whole,
                whole,
            ],
            out_specs=pl.BlockSpec((rows, 1, cells, bins), lambda v: (0, v, 0, 0)),
            out_shape=jax.ShapeDtypeStruct((rows, items, cells, bins), jnp.bfloat16),
            compiler_params=params,
        )(dens, top, bottom, mix, mix_top, mix_bottom)

    return jax.shard_map(
        shards,
        mesh=mesh,
        in_specs=(P("member", "band", None, None), P("member", "band", None), P(), P()),
        out_specs=P("band", None, "member", None),
        check_vma=False,
    )
```

time: 104 us -> 57.9 us (0.56)
  waiting for transfers between devices: 28.7 us -> 0 us
  local copies, waits for them, and re-layouts: 21 us -> 6.28 us
  starting transfers between devices: 11.8 us -> 0 us
  Pallas kernels: 40.6 us -> 50.1 us
    all_to_all x1 -> x0, waiting for transfers between devices: 20.5 us -> none  [shards(): lax.all_to_all(values, 'member', split_axis=0, concat_axis=0, tiled=True)]
    pallas_call x2 -> x1, Pallas kernels: 32.2 us -> 41.6 us  [shards(): pl.pallas_call(functools.partial(density_kernel, n, count, cells, width,...]
    ppermute x2 -> x0, waiting for transfers between devices: 8.22 us -> none  [the longest x1 5.5 us: shards(): bottom = lax.ppermute(head, 'band', [(i + 1, i) for i in range(count - 1)])]
    ppermute x2 -> x0, starting transfers between devices: 6.35 us -> none  [the longest x1 4.44 us: shards(): top = lax.ppermute(tail, 'band', [(i, i + 1) for i in range(count - 1)])]
    slice x3 -> x0, local copies, waits for them, and re-layouts: 6.31 us -> none  [the longest x2 4.09 us: shards(): head = dens[:, :, :edge]]
    all_to_all x1 -> x0, starting transfers between devices: 5.42 us -> none  [shards(): lax.all_to_all(values, 'member', split_axis=0, concat_axis=0, tiled=True)]
    unnamed x21 -> x12, local copies, waits for them, and re-layouts: 9.91 us -> 6.28 us
    ppermute x2 -> x0, local copies, waits for them, and re-layouts: 3.53 us -> none  [the longest x1 2.21 us: shards(): top = lax.ppermute(tail, 'band', [(i, i + 1) for i in range(count - 1)])]
  transfers between devices with their start and end apart: 3 -> 0, of which waited for: 3 -> 0; matrix products, arithmetic and copies ran while one was open for 5% -> 0% of each run, Pallas kernels for 0% -> 0%
where the time goes in v2:
time: 57.9 us; the launch traced here: 57.2 us
  Pallas kernels  50.1 us (87%)
  local copies, waits for them, and re-layouts  6.28 us (11%)
  other arithmetic  0.81 us (1%)
    pallas_call x1, Pallas kernels, shards(): pl.pallas_call(functools.partial(density_kernel, n, count, cells, width,...  41.6 us
    pallas_call x1, Pallas kernels, shards(): pl.pallas_call(functools.partial(window_kernel, rows, cells), grid=(items...  8.49 us
    unnamed x12, local copies, waits for them, and re-layouts  6.28 us

profile of v2, /device:TPU:1, one launch (start us, length us, event | category | flops | bytes accessed | tf_op | source)
XLA Modules:
  0.0 57.2 jit_solution(540371388642059321)
XLA Ops:
  0.0 0.8 %multiply_bitcast_fusion.scale_ref = f32[6,16,12]{2,1,0:T(8,128)S(1)} fusion(s32[16,12,6]{1,0,2:T(8,128)} %param.8), kind=kLoop, calls=%fused_computation | loop fusion | flops 4608 | bytes 9216 | tf_op jit(solution)/shard_map/transpose | solution.py:278
  0.8 0.0 copy-start.1
  0.8 1.5 %copy-done.1 = s32[16,12,6,352]{3,0,2,1:T(8,128)S(1)} copy-done((s32[16,12,6,352]{3,0,2,1:T(8,128)S(1)}, s32[16,12,6,352]{3,0,2,1:T(8,128)}, u32[]{:S(2)}) %copy-start.1) | copy-done | bytes 1622040
  2.3 0.0 copy-start.4
  2.3 0.7 %copy-done.4 = f32[6,256]{1,0:T(8,128)S(1)} copy-done((f32[6,256]{1,0:T(8,128)S(1)}, f32[6,256]{1,0:T(8,128)}, u32[]{:S(2)}) %copy-start.4) | copy-done | bytes 6168
  3.0 0.0 copy-start.5
  3.0 0.7 %copy-done.5 = f32[6]{0:T(128)S(1)} copy-done((f32[6]{0:T(128)S(1)}, f32[6]{0:T(128)}, u32[]{:S(2)}) %copy-start.5) | copy-done | bytes 48
  3.6 41.6 %shard_map.73 = (bf16[6,256,1152]{2,1,0:T(8,128)(2,1)}, bf16[6,256,256]{2,1,0:T(8,128)(2,1)S(1)}, bf16[6,256,256]{2,1,0:T(8,128)(2,1)S(1)}) custom-call(s32[12,6,16,352]{3,2,1,0:T(8,128)S(1)} %bitcast.3, f32[6,16,12]{2,1,0:T(8,128)S(1)} %multiply_bitcast_fusion.scale_ref, f32[6,256]{1,0:T(8,128)S(1)} %copy-done.4, f32[6]{0:T(128)S(1)} %copy-done.5), custom_call_target="tpu_custom_call" | custom-call | tf_op jit(solution)/shard_map/pallas_call | solution.py:285
  45.2 0.0 copy-start
  45.3 1.7 %copy-done = bf16[1056,1152]{1,0:T(8,128)(2,1)S(1)} copy-done((bf16[1056,1152]{1,0:T(8,128)(2,1)S(1)}, bf16[1056,1152]{1,0:T(8,128)(2,1)}, u32[]{:S(2)}) %copy-start) | copy-done | bytes 2433048
  46.9 0.0 copy-start.2
  46.9 0.9 %copy-done.2 = bf16[176,256]{1,0:T(8,128)(2,1)S(1)} copy-done((bf16[176,256]{1,0:T(8,128)(2,1)S(1)}, bf16[176,256]{1,0:T(8,128)(2,1)}, u32[]{:S(2)}) %copy-start.2) | copy-done | bytes 90136
  47.8 0.0 copy-start.3
  47.8 0.9 %copy-done.3 = bf16[176,256]{1,0:T(8,128)(2,1)S(1)} copy-done((bf16[176,256]{1,0:T(8,128)(2,1)S(1)}, bf16[176,256]{1,0:T(8,128)(2,1)}, u32[]{:S(2)}) %copy-start.3) | copy-done | bytes 90136
  48.7 8.5 %shard_map.74 = bf16[12,6,88,256]{3,2,1,0:T(8,128)(2,1)} custom-call(bf16[6,256,1152]{2,1,0:T(8,128)(2,1)} %get-tuple-element.8.own_ref, bf16[6,256,256]{2,1,0:T(8,128)(2,1)S(1)} %get-tuple-element.9.top_ref, bf16[6,256,256]{2,1,0:T(8,128)(2,1)S(1)} %get-tuple-element.10.bottom_ref, bf16[1056,1152]{1,0:T(8,128)(2,1)S(1)} %copy-done, ...), custom_call_target="tpu_custom_call" | custom-call | tf_op jit(solution)/shard_map/pallas_call | solution.py:319
Async XLA Ops:
  0.8 1.5 %copy-start.1 = (s32[16,12,6,352]{3,0,2,1:T(8,128)S(1)}, s32[16,12,6,352]{3,0,2,1:T(8,128)}, u32[]{:S(2)}) copy-start(s32[16,12,6,352]{3,0,2,1:T(8,128)} %param.7) | copy-start | bytes 4866052
  2.3 0.7 %copy-start.4 = (f32[6,256]{1,0:T(8,128)S(1)}, f32[6,256]{1,0:T(8,128)}, u32[]{:S(2)}) copy-start(f32[6,256]{1,0:T(8,128)} %centers_ref.1) | copy-start | bytes 18436
  3.0 0.7 %copy-start.5 = (f32[6]{0:T(128)S(1)}, f32[6]{0:T(128)}, u32[]{:S(2)}) copy-start(f32[6]{0:T(128)} %widths_ref.1) | copy-start | bytes 76
  45.2 1.7 %copy-start = (bf16[1056,1152]{1,0:T(8,128)(2,1)S(1)}, bf16[1056,1152]{1,0:T(8,128)(2,1)}, u32[]{:S(2)}) copy-start(bf16[1056,1152]{1,0:T(8,128)(2,1)} %constant.12.clone.mix_ref) | copy-start | bytes 7299076
  46.9 0.9 %copy-start.2 = (bf16[176,256]{1,0:T(8,128)(2,1)S(1)}, bf16[176,256]{1,0:T(8,128)(2,1)}, u32[]{:S(2)}) copy-start(bf16[176,256]{1,0:T(8,128)(2,1)} %constant.14.clone.mix_bottom_ref) | copy-start | bytes 270340
  47.8 0.9 %copy-start.3 = (bf16[176,256]{1,0:T(8,128)(2,1)S(1)}, bf16[176,256]{1,0:T(8,128)(2,1)}, u32[]{:S(2)}) copy-start(bf16[176,256]{1,0:T(8,128)(2,1)} %constant.13.clone.mix_top_ref) | copy-start | bytes 270340

commit v3 on v2

--- a/solution.py
+++ b/solution.py
@@ -17,27 +17,33 @@
 POINTS = 2 * HALF
 FIELDS = 16
 WORDS = POINTS // FIELDS
-VMEM = 48 * 1024 * 1024
-
-
-def regroup(codes_ref, scale_ref, v, n, cells, width):
+VMEM = 60 * 1024 * 1024
+AHEAD = 2
+
+
+def regroup(codes_ref, exponents_ref, v, n, cells, width):
     rows, _, members, _ = codes_ref.shape
     wide = cells + 2 * REACH
+    lon = codes_ref.shape[3]
     edge = jnp.full((members, REACH), OUTSIDE, jnp.float32)
     rest = jnp.full((members, width - rows * wide), OUTSIDE, jnp.float32)
-    lines = []
-    for r in range(rows):
-        line = codes_ref[r, v].astype(jnp.float32)
-        line = line * scale_ref[v, :, r : r + 1]
-        lines.append(jnp.concatenate([edge, line, edge], axis=1))
+    scale = jnp.left_shift(1, exponents_ref[v] + 8).astype(jnp.float32) * (1.0 / FINE)
+    lines = [codes_ref[r, v].astype(jnp.float32) * scale[:, r : r + 1] for r in range(rows)]
     for d in range(n):
-        parts = [line[:, d * cells : d * cells + wide] for line in lines]
+        low, high = d * cells - REACH, (d + 1) * cells + REACH
+        parts = []
+        for line in lines:
+            if low < 0:
+                parts.append(edge)
+            parts.append(line[:, max(low, 0) : min(high, lon)])
+            if high > lon:
+                parts.append(edge)
         yield d, jnp.concatenate(parts + [rest], axis=1).astype(jnp.bfloat16)
 
 
 def density_kernel(
     n, count, cells, width, lead, trail,
-    codes_ref, scale_ref, centers_ref, widths_ref,
+    codes_ref, exponents_ref, centers_ref, widths_ref,
     own_ref, top_ref, bottom_ref,
     send, recv, dens, zeros, table, words, steps, counts, bytes4,
     send_sem, recv_sem, up_sem, down_sem, own_sem, zero_sem,
@@ -101,13 +107,14 @@
         return pltpu.make_async_copy(dens.at[v], own_ref.at[v], own_sem.at[v])
 
     for v in range(items):
-        for d, block in regroup(codes_ref, scale_ref, v, n, cells, width):
+        for d, block in regroup(codes_ref, exponents_ref, v, n, cells, width):
             send[v, d] = block
         if v == 0:
             beside = jnp.where(band > 0, 1, 0) + jnp.where(band < count - 1, 1, 0)
             pl.semaphore_wait(barrier, n - 1 + beside)
-        for o in range(1, n):
-            outgoing(v, o).start()
+        if v < AHEAD:
+            for o in range(1, n):
+                outgoing(v, o).start()
 
     zeros[...] = jnp.zeros_like(zeros)
 
@@ -133,13 +140,22 @@
         cross = lax.broadcasted_iota(jnp.int32, (bins, bins), 0) == lax.broadcasted_iota(jnp.int32, (bins, bins), 1)
         center = jnp.sum(jnp.where(cross, centers_ref[pl.ds(v, 1), :], 0.0), axis=1, keepdims=True)
         scaled = (center - value) / wide
-        table[...] = jnp.exp(-0.5 * scaled * scaled).astype(jnp.bfloat16)
+        norm = 1.0 / (total * wide * math.sqrt(2.0 * math.pi))
+        table[...] = (jnp.exp(-0.5 * scaled * scaled) * norm).astype(jnp.bfloat16)
+
+        for o in range(1, n):
+            outgoing(v, o).wait_recv()
+
+        @pl.when(v + AHEAD < items)
+        def _():
+            for o in range(1, n):
+                outgoing(v + AHEAD, o).start()
+
 
         for i in range(n):
             if i == 0:
                 vals = send[v, me]
             else:
-                outgoing(v, i).wait_recv()
                 vals = recv[v, i - 1]
             vals = vals.astype(jnp.float32) * FINE
             size = jnp.abs(vals).astype(jnp.int32)
@@ -152,12 +168,10 @@
             words[i * members : (i + 1) * members] = jnp.where(there, index - WORDS * field, WORDS)
             steps[i * members : (i + 1) * members] = jnp.left_shift(1, jnp.where(there, 2 * field, 0))
 
-        norm = 1.0 / (total * wide * math.sqrt(2.0 * math.pi))
-
         def finish(g):
             part = jnp.dot(table[...], counts[...], preferred_element_type=jnp.float32)
             at = pl.ds(pl.multiple_of(g * lanes, lanes), lanes)
-            dens[v, :, at] = (part * norm).astype(jnp.bfloat16)
+            dens[v, :, at] = part.astype(jnp.bfloat16)
 
         def group(g, _):
             finish(jnp.maximum(g - 1, 0))
@@ -235,22 +249,24 @@
             blank(v, 1).wait()
 
 
-def window_kernel(rows, cells, own_ref, top_ref, bottom_ref, mix_ref, mix_top_ref, mix_bottom_ref, out_ref):
+def window_kernel(rows, cells, chunks, own_ref, top_ref, bottom_ref, mix_ref, mix_top_ref, mix_bottom_ref, out_ref):
     edge = mix_top_ref.shape[0]
     dims = (((1,), (1,)), ((), ()))
     def mixed(mix, dens):
         return lax.dot_general(mix, dens, dims, preferred_element_type=jnp.float32)
     above = mixed(mix_top_ref[...], top_ref[0])
     below = mixed(mix_bottom_ref[...], bottom_ref[0])
-    full = mixed(mix_ref[...], own_ref[0])
-    for r in range(rows):
-        part = full[r * cells : (r + 1) * cells]
-        if r < REACH:
-            part = part + above[r * cells : (r + 1) * cells]
-        if r >= rows - REACH:
-            at = edge - (rows - r) * cells
-            part = part + below[at : at + cells]
-        out_ref[r, 0] = (part / 25.0).astype(jnp.bfloat16)
+    for c, (first, low, high) in enumerate(chunks):
+        size = mix_ref.shape[1] // cells
+        full = mixed(mix_ref[c, :, : high - low], own_ref[0, :, low:high])
+        for r in range(first, first + size):
+            part = full[(r - first) * cells : (r - first + 1) * cells]
+            if r < REACH:
+                part = part + above[r * cells : (r + 1) * cells]
+            if r >= rows - REACH:
+                at = edge - (rows - r) * cells
+                part = part + below[at : at + cells]
+            out_ref[r, 0] = (part / 25.0).astype(jnp.bfloat16)
 
 
 def window(rows, first, cells, lanes, source_rows, source_first):
@@ -261,7 +277,7 @@
     dl = place[None, :] - (out % cells)[:, None]
     real = (row >= source_rows[0]) & (row < source_rows[1])
     inside = (dr <= REACH) & (dl >= 0) & (dl <= 2 * REACH) & real[None, :]
-    return jnp.asarray(inside, jnp.bfloat16)
+    return inside.astype(jnp.bfloat16)
 
 
 def solution(mesh):
@@ -274,8 +290,7 @@
         cells = lon // n
         wide = cells + 2 * REACH
         width = -(-rows * wide // 128) * 128
-        scale = jnp.left_shift(1, exponents + 8).astype(jnp.float32) * (1.0 / FINE)
-        scale = jnp.transpose(scale, (2, 0, 1))
+        exponents = jnp.transpose(exponents, (2, 0, 1))
         codes = jnp.transpose(codes, (1, 2, 0, 3))
         lead = -(-REACH * wide // 128) * 128
         trail = width - (rows - REACH) * wide // 128 * 128
@@ -311,13 +326,22 @@
             compiler_params=pltpu.CompilerParams(
                 vmem_limit_bytes=VMEM, collective_id=0, has_side_effects=True
             ),
-        )(codes, scale, centers, widths)
-        mix = window(rows, 0, cells, np.arange(width), (0, rows), 0)
+        )(codes, exponents, centers, widths)
+        size = max(k for k in (3, 2, 1) if rows % k == 0)
+        chunks = []
+        for first in range(0, rows, size):
+            low = max(first - REACH, 0) * wide // 128 * 128
+            high = -(-min(first + size + REACH, rows) * wide // 128) * 128
+            chunks.append((first, low, high))
+        depth = max(high - low for _, low, high in chunks)
+        mix = np.stack(
+            [window(size, first, cells, np.arange(low, low + depth), (0, rows), 0) for first, low, _ in chunks]
+        )
         mix_top = window(REACH, 0, cells, np.arange(width - trail, width), (rows - REACH, rows), -rows)
         mix_bottom = window(REACH, rows - REACH, cells, np.arange(lead), (0, REACH), rows)
         whole = pl.BlockSpec(memory_space=pltpu.VMEM)
         return pl.pallas_call(
-            functools.partial(window_kernel, rows, cells),
+            functools.partial(window_kernel, rows, cells, chunks),
             grid=(items,),
             in_specs=[
                 pl.BlockSpec((1, bins, width), lambda v: (v, 0, 0)),

time: 57.9 us -> 51.2 us (0.88)
  local copies, waits for them, and re-layouts: 6.28 us -> 0 us
  other arithmetic: 0.81 us -> 0 us
  Pallas kernels: 50.1 us -> 50.7 us
    unnamed x12 -> x0, local copies, waits for them, and re-layouts: 6.28 us -> none
    pallas_call x1, Pallas kernels: 41.6 us -> 42.6 us  [shards(): pl.pallas_call(functools.partial(density_kernel, n, count, cells, width,...]
    transpose x1 -> x0, other arithmetic: 0.81 us -> none  [shards(): scale = jnp.transpose(scale, (2, 0, 1))]
where the time goes in v3:
time: 51.2 us; the launch traced here: 50.7 us
  Pallas kernels  50.7 us (99%)
    pallas_call x1, Pallas kernels, shards(): pl.pallas_call(functools.partial(density_kernel, n, count, cells, width,...  42.6 us
    pallas_call x1, Pallas kernels, shards(): pl.pallas_call(functools.partial(window_kernel, rows, cells, chunks), gri...  8.07 us

profile of v3, /device:TPU:1, one launch (start us, length us, event | category | flops | bytes accessed | tf_op | source)
XLA Modules:
  0.0 50.7 jit_solution(18365400914405716239)
XLA Ops:
  0.0 42.6 %shard_map.73 = (bf16[6,256,1152]{2,1,0:T(8,128)(2,1)}, bf16[6,256,256]{2,1,0:T(8,128)(2,1)}, bf16[6,256,256]{2,1,0:T(8,128)(2,1)}) custom-call(s32[12,6,16,352]{3,2,1,0:T(8,128)} %bitcast.2, s32[6,16,12]{2,1,0:T(8,128)} %bitcast.3, f32[6,256]{1,0:T(8,128)} %centers_ref.1, f32[6]{0:T(128)} %widths_ref.1), custom_call_target="tpu_custom_call" | custom-call | tf_op jit(solution)/shard_map/pallas_call | solution.py:300
  42.6 8.1 %shard_map.74 = bf16[12,6,88,256]{3,2,1,0:T(8,128)(2,1)} custom-call(bf16[6,256,1152]{2,1,0:T(8,128)(2,1)} %get-tuple-element.8.own_ref, bf16[6,256,256]{2,1,0:T(8,128)(2,1)} %get-tuple-element.9.top_ref, bf16[6,256,256]{2,1,0:T(8,128)(2,1)} %get-tuple-element.10.bottom_ref, bf16[4,264,768]{2,1,0:T(8,128)(2,1)} %constant.6.clone.mix_ref, ...), custom_call_target="tpu_custom_call" | custom-call | tf_op jit(solution)/shard_map/pallas_call | solution.py:343

commit v4 on v3

--- a/solution.py
+++ b/solution.py
@@ -42,7 +42,7 @@
 
 
 def density_kernel(
-    n, count, cells, width, lead, trail,
+    n, count, cells, width, lead, after, trail,
     codes_ref, exponents_ref, centers_ref, widths_ref,
     own_ref, top_ref, bottom_ref,
     send, recv, dens, zeros, table, words, steps, counts, bytes4,
@@ -53,6 +53,8 @@
     bins = centers_ref.shape[1]
     lanes = 128
     groups = width // lanes
+    front = -(-lead // lanes)
+    back = min(groups - after // lanes, groups - front)
     me = lax.axis_index("member")
     band = lax.axis_index("band")
 
@@ -80,7 +82,7 @@
 
     def upward(v):
         return pltpu.make_async_remote_copy(
-            src_ref=dens.at[v, :, pl.ds(width - trail, trail)],
+            src_ref=dens.at[v, pl.ds(after, trail)],
             dst_ref=top_ref.at[v],
             send_sem=up_sem.at[v, 0],
             recv_sem=up_sem.at[v, 1],
@@ -90,7 +92,7 @@
 
     def downward(v):
         return pltpu.make_async_remote_copy(
-            src_ref=dens.at[v, :, pl.ds(0, lead)],
+            src_ref=dens.at[v, pl.ds(0, lead)],
             dst_ref=bottom_ref.at[v],
             send_sem=down_sem.at[v, 0],
             recv_sem=down_sem.at[v, 1],
@@ -100,8 +102,8 @@
 
     def blank(v, side):
         if side == 0:
-            return pltpu.make_async_copy(zeros.at[:, pl.ds(0, trail)], top_ref.at[v], zero_sem.at[0, v])
-        return pltpu.make_async_copy(zeros.at[:, pl.ds(0, lead)], bottom_ref.at[v], zero_sem.at[1, v])
+            return pltpu.make_async_copy(zeros.at[pl.ds(0, trail)], top_ref.at[v], zero_sem.at[0, v])
+        return pltpu.make_async_copy(zeros.at[pl.ds(0, lead)], bottom_ref.at[v], zero_sem.at[1, v])
 
     def keep(v):
         return pltpu.make_async_copy(dens.at[v], own_ref.at[v], own_sem.at[v])
@@ -171,10 +173,15 @@
         def finish(g):
             part = jnp.dot(table[...], counts[...], preferred_element_type=jnp.float32)
             at = pl.ds(pl.multiple_of(g * lanes, lanes), lanes)
-            dens[v, :, at] = part.astype(jnp.bfloat16)
-
-        def group(g, _):
-            finish(jnp.maximum(g - 1, 0))
+            dens[v, at] = jnp.transpose(part).astype(jnp.bfloat16)
+
+        def place(i):
+            spot = jnp.where(i < front + back, groups - back + i - front, i - back)
+            return jnp.where(i < front, i, spot)
+
+        def group(i, _, first):
+            finish(place(jnp.maximum(i - 1, first)))
+            g = place(i)
             at = pl.ds(pl.multiple_of(g * lanes, lanes), lanes)
             row = lax.broadcasted_iota(jnp.int32, (WORDS, lanes), 0)
             for start in range(0, total, 15):
@@ -205,9 +212,8 @@
                 counts[f * WORDS : (f + 1) * WORDS] = part.astype(jnp.float32).astype(jnp.bfloat16)
             return 0
 
-        lax.fori_loop(0, groups, group, 0)
-        finish(groups - 1)
-        keep(v).start()
+        lax.fori_loop(0, front + back, functools.partial(group, first=0), 0)
+        finish(place(front + back - 1))
 
         @pl.when(band > 0)
         def _():
@@ -217,6 +223,10 @@
         def _():
             upward(v).start()
 
+        if front + back < groups:
+            lax.fori_loop(front + back, groups, functools.partial(group, first=front + back), 0)
+            finish(place(groups - 1))
+        keep(v).start()
         return 0
 
     lax.fori_loop(0, items, item, 0)
@@ -251,14 +261,14 @@
 
 def window_kernel(rows, cells, chunks, own_ref, top_ref, bottom_ref, mix_ref, mix_top_ref, mix_bottom_ref, out_ref):
     edge = mix_top_ref.shape[0]
-    dims = (((1,), (1,)), ((), ()))
+    dims = (((1,), (0,)), ((), ()))
     def mixed(mix, dens):
         return lax.dot_general(mix, dens, dims, preferred_element_type=jnp.float32)
     above = mixed(mix_top_ref[...], top_ref[0])
     below = mixed(mix_bottom_ref[...], bottom_ref[0])
     for c, (first, low, high) in enumerate(chunks):
         size = mix_ref.shape[1] // cells
-        full = mixed(mix_ref[c, :, : high - low], own_ref[0, :, low:high])
+        full = mixed(mix_ref[c, :, : high - low], own_ref[0, low:high])
         for r in range(first, first + size):
             part = full[(r - first) * cells : (r - first + 1) * cells]
             if r < REACH:
@@ -266,7 +276,7 @@
             if r >= rows - REACH:
                 at = edge - (rows - r) * cells
                 part = part + below[at : at + cells]
-            out_ref[r, 0] = (part / 25.0).astype(jnp.bfloat16)
+            out_ref[r, 0] = (part * (1.0 / 25.0)).astype(jnp.bfloat16)
 
 
 def window(rows, first, cells, lanes, source_rows, source_first):
@@ -292,25 +302,26 @@
         width = -(-rows * wide // 128) * 128
         exponents = jnp.transpose(exponents, (2, 0, 1))
         codes = jnp.transpose(codes, (1, 2, 0, 3))
-        lead = -(-REACH * wide // 128) * 128
-        trail = width - (rows - REACH) * wide // 128 * 128
+        lead = -(-REACH * wide // 16) * 16
+        after = (rows - REACH) * wide // 16 * 16
+        trail = -(-(rows * wide - after) // 16) * 16
         params = pltpu.CompilerParams(vmem_limit_bytes=VMEM)
         vmem = pl.BlockSpec(memory_space=pltpu.VMEM)
         hbm = pl.BlockSpec(memory_space=pl.ANY)
         dens, top, bottom = pl.pallas_call(
-            functools.partial(density_kernel, n, count, cells, width, lead, trail),
+            functools.partial(density_kernel, n, count, cells, width, lead, after, trail),
             in_specs=[vmem, vmem, vmem, pl.BlockSpec(memory_space=pltpu.SMEM)],
             out_specs=[hbm, hbm, hbm],
             out_shape=[
-                jax.ShapeDtypeStruct((items, bins, width), jnp.bfloat16),
-                jax.ShapeDtypeStruct((items, bins, trail), jnp.bfloat16),
-                jax.ShapeDtypeStruct((items, bins, lead), jnp.bfloat16),
+                jax.ShapeDtypeStruct((items, width, bins), jnp.bfloat16),
+                jax.ShapeDtypeStruct((items, trail, bins), jnp.bfloat16),
+                jax.ShapeDtypeStruct((items, lead, bins), jnp.bfloat16),
             ],
             scratch_shapes=[
                 pltpu.VMEM((items, n, members, width), jnp.bfloat16),
                 pltpu.VMEM((items, max(n - 1, 1), members, width), jnp.bfloat16),
-                pltpu.VMEM((items, bins, width), jnp.bfloat16),
-                pltpu.VMEM((bins, max(lead, trail)), jnp.bfloat16),
+                pltpu.VMEM((items, width, bins), jnp.bfloat16),
+                pltpu.VMEM((max(lead, trail), bins), jnp.bfloat16),
                 pltpu.VMEM((bins, POINTS), jnp.bfloat16),
                 pltpu.VMEM((n * members, width), jnp.int32),
                 pltpu.VMEM((n * members, width), jnp.int32),
@@ -337,16 +348,16 @@
         mix = np.stack(
             [window(size, first, cells, np.arange(low, low + depth), (0, rows), 0) for first, low, _ in chunks]
         )
-        mix_top = window(REACH, 0, cells, np.arange(width - trail, width), (rows - REACH, rows), -rows)
+        mix_top = window(REACH, 0, cells, np.arange(after, after + trail), (rows - REACH, rows), -rows)
         mix_bottom = window(REACH, rows - REACH, cells, np.arange(lead), (0, REACH), rows)
         whole = pl.BlockSpec(memory_space=pltpu.VMEM)
         return pl.pallas_call(
             functools.partial(window_kernel, rows, cells, chunks),
             grid=(items,),
             in_specs=[
-                pl.BlockSpec((1, bins, width), lambda v: (v, 0, 0)),
-                pl.BlockSpec((1, bins, trail), lambda v: (v, 0, 0)),
-                pl.BlockSpec((1, bins, lead), lambda v: (v, 0, 0)),
+                pl.BlockSpec((1, width, bins), lambda v: (v, 0, 0)),
+                pl.BlockSpec((1, trail, bins), lambda v: (v, 0, 0)),
+                pl.BlockSpec((1, lead, bins), lambda v: (v, 0, 0)),
                 whole,
                 whole,
                 whole,

time: 51.2 us -> 53.9 us (1.053)
  Pallas kernels: 50.7 us -> 53.3 us
    pallas_call x1, Pallas kernels: 42.6 us -> 45.7 us  [shards(): pl.pallas_call(functools.partial(density_kernel, n, count, cells, width,...]
where the time goes in v4:
time: 53.9 us; the launch traced here: 53.3 us
  Pallas kernels  53.3 us (99%)
    pallas_call x1, Pallas kernels, shards(): pl.pallas_call(functools.partial(density_kernel, n, count, cells, width,...  45.7 us
    pallas_call x1, Pallas kernels, shards(): pl.pallas_call(functools.partial(window_kernel, rows, cells, chunks), gri...  7.61 us

profile of v4, /device:TPU:1, one launch (start us, length us, event | category | flops | bytes accessed | tf_op | source)
XLA Modules:
  0.0 53.3 jit_solution(3604520778878450992)
XLA Ops:
  0.0 45.7 %shard_map.73 = (bf16[6,1152,256]{2,1,0:T(8,128)(2,1)}, bf16[6,192,256]{2,1,0:T(8,128)(2,1)}, bf16[6,192,256]{2,1,0:T(8,128)(2,1)}) custom-call(s32[12,6,16,352]{3,2,1,0:T(8,128)} %bitcast.2, s32[6,16,12]{2,1,0:T(8,128)} %bitcast.3, f32[6,256]{1,0:T(8,128)} %centers_ref.1, f32[6]{0:T(128)} %widths_ref.1), custom_call_target="tpu_custom_call" | custom-call | tf_op jit(solution)/shard_map/pallas_call | solution.py:311
  45.7 7.6 %shard_map.74 = bf16[12,6,88,256]{3,2,1,0:T(8,128)(2,1)} custom-call(bf16[6,1152,256]{2,1,0:T(8,128)(2,1)} %get-tuple-element.8.own_ref, bf16[6,192,256]{2,1,0:T(8,128)(2,1)} %get-tuple-element.9.top_ref, bf16[6,192,256]{2,1,0:T(8,128)(2,1)} %get-tuple-element.10.bottom_ref, bf16[4,264,768]{2,1,0:T(8,128)(2,1)} %constant.6.clone.mix_ref, ...), custom_call_target="tpu_custom_call" | custom-call | tf_op jit(solution)/shard_map/pallas_call | solution.py:354

commit v5 on v3

--- a/solution.py
+++ b/solution.py
@@ -53,6 +53,8 @@
     bins = centers_ref.shape[1]
     lanes = 128
     groups = width // lanes
+    front = lead // lanes
+    back = min(trail // lanes, groups - front)
     me = lax.axis_index("member")
     band = lax.axis_index("band")
 
@@ -127,8 +129,6 @@
     def _():
         for v in range(items):
             blank(v, 1).start()
-
-    counts[...] = jnp.zeros_like(counts)
 
     def item(v, _):
         wide = widths_ref[v]
@@ -168,13 +168,13 @@
             words[i * members : (i + 1) * members] = jnp.where(there, index - WORDS * field, WORDS)
             steps[i * members : (i + 1) * members] = jnp.left_shift(1, jnp.where(there, 2 * field, 0))
 
-        def finish(g):
-            part = jnp.dot(table[...], counts[...], preferred_element_type=jnp.float32)
-            at = pl.ds(pl.multiple_of(g * lanes, lanes), lanes)
-            dens[v, :, at] = part.astype(jnp.bfloat16)
-
-        def group(g, _):
-            finish(jnp.maximum(g - 1, 0))
+        def finish(low, high):
+            part = jnp.dot(table[...], counts[:, low:high], preferred_element_type=jnp.float32)
+            dens[v, :, low:high] = part.astype(jnp.bfloat16)
+
+        def group(i, _):
+            spot = jnp.where(i < front + back, groups - back + i - front, i - back)
+            g = jnp.where(i < front, i, spot)
             at = pl.ds(pl.multiple_of(g * lanes, lanes), lanes)
             row = lax.broadcasted_iota(jnp.int32, (WORDS, lanes), 0)
             for start in range(0, total, 15):
@@ -202,12 +202,12 @@
                 part = lax.shift_right_logical(bytes4[f % 4], 8 * (f // 4))
                 if f // 4 < 3:
                     part = part & 0xFF
-                counts[f * WORDS : (f + 1) * WORDS] = part.astype(jnp.float32).astype(jnp.bfloat16)
+                counts[f * WORDS : (f + 1) * WORDS, at] = part.astype(jnp.float32).astype(jnp.bfloat16)
             return 0
 
-        lax.fori_loop(0, groups, group, 0)
-        finish(groups - 1)
-        keep(v).start()
+        lax.fori_loop(0, front + back, group, 0)
+        finish(0, front * lanes)
+        finish((groups - back) * lanes, groups * lanes)
 
         @pl.when(band > 0)
         def _():
@@ -217,6 +217,10 @@
         def _():
             upward(v).start()
 
+        if front + back < groups:
+            lax.fori_loop(front + back, groups, group, 0)
+            finish(front * lanes, (groups - back) * lanes)
+        keep(v).start()
         return 0
 
     lax.fori_loop(0, items, item, 0)
@@ -266,7 +270,7 @@
             if r >= rows - REACH:
                 at = edge - (rows - r) * cells
                 part = part + below[at : at + cells]
-            out_ref[r, 0] = (part / 25.0).astype(jnp.bfloat16)
+            out_ref[r, 0] = (part * (1.0 / 25.0)).astype(jnp.bfloat16)
 
 
 def window(rows, first, cells, lanes, source_rows, source_first):
@@ -314,7 +318,7 @@
                 pltpu.VMEM((bins, POINTS), jnp.bfloat16),
                 pltpu.VMEM((n * members, width), jnp.int32),
                 pltpu.VMEM((n * members, width), jnp.int32),
-                pltpu.VMEM((POINTS, 128), jnp.bfloat16),
+                pltpu.VMEM((POINTS, width), jnp.bfloat16),
                 pltpu.VMEM((4, WORDS, 128), jnp.int32),
                 pltpu.SemaphoreType.DMA((items, n)),
                 pltpu.SemaphoreType.DMA((items, n)),

time: 51.2 us -> 49.7 us (0.971)
  Pallas kernels: 50.7 us -> 49 us
    pallas_call x1, Pallas kernels: 42.6 us -> 40.9 us  [shards(): pl.pallas_call(functools.partial(density_kernel, n, count, cells, width,...]
where the time goes in v5:
time: 49.7 us; the launch traced here: 49 us
  Pallas kernels  49 us (99%)
    pallas_call x1, Pallas kernels, shards(): pl.pallas_call(functools.partial(density_kernel, n, count, cells, width,...  40.9 us
    pallas_call x1, Pallas kernels, shards(): pl.pallas_call(functools.partial(window_kernel, rows, cells, chunks), gri...  8.07 us

profile of v5, /device:TPU:1, one launch (start us, length us, event | category | flops | bytes accessed | tf_op | source)
XLA Modules:
  0.0 49.0 jit_solution(17060362091528717462)
XLA Ops:
  0.0 40.9 %shard_map.73 = (bf16[6,256,1152]{2,1,0:T(8,128)(2,1)}, bf16[6,256,256]{2,1,0:T(8,128)(2,1)}, bf16[6,256,256]{2,1,0:T(8,128)(2,1)}) custom-call(s32[12,6,16,352]{3,2,1,0:T(8,128)} %bitcast.2, s32[6,16,12]{2,1,0:T(8,128)} %bitcast.3, f32[6,256]{1,0:T(8,128)} %centers_ref.1, f32[6]{0:T(128)} %widths_ref.1), custom_call_target="tpu_custom_call" | custom-call | tf_op jit(solution)/shard_map/pallas_call | solution.py:304
  41.0 8.1 %shard_map.74 = bf16[12,6,88,256]{3,2,1,0:T(8,128)(2,1)} custom-call(bf16[6,256,1152]{2,1,0:T(8,128)(2,1)} %get-tuple-element.8.own_ref, bf16[6,256,256]{2,1,0:T(8,128)(2,1)} %get-tuple-element.9.top_ref, bf16[6,256,256]{2,1,0:T(8,128)(2,1)} %get-tuple-element.10.bottom_ref, bf16[4,264,768]{2,1,0:T(8,128)(2,1)} %constant.6.clone.mix_ref, ...), custom_call_target="tpu_custom_call" | custom-call | tf_op jit(solution)/shard_map/pallas_call | solution.py:347

commit v6 on v5

--- a/solution.py
+++ b/solution.py
@@ -18,7 +18,7 @@
 FIELDS = 16
 WORDS = POINTS // FIELDS
 VMEM = 60 * 1024 * 1024
-AHEAD = 2
+AHEAD = 3
 
 
 def regroup(codes_ref, exponents_ref, v, n, cells, width):
@@ -205,7 +205,7 @@
                 counts[f * WORDS : (f + 1) * WORDS, at] = part.astype(jnp.float32).astype(jnp.bfloat16)
             return 0
 
-        lax.fori_loop(0, front + back, group, 0)
+        lax.fori_loop(0, front + back, group, 0, unroll=2)
         finish(0, front * lanes)
         finish((groups - back) * lanes, groups * lanes)
 

time: 49.7 us -> 50.3 us (1.012)
  the two profiles are of different devices: /device:TPU:1 before, /device:TPU:9 now
where the time goes in v6:
time: 50.3 us; the launch traced here: 50.1 us
  Pallas kernels  50.1 us (100%)
    pallas_call x1, Pallas kernels, shards(): pl.pallas_call(functools.partial(density_kernel, n, count, cells, width,...  42 us
    pallas_call x1, Pallas kernels, shards(): pl.pallas_call(functools.partial(window_kernel, rows, cells, chunks), gri...  8.07 us

profile of v6, /device:TPU:9, one launch (start us, length us, event | category | flops | bytes accessed | tf_op | source)
XLA Modules:
  0.0 50.1 jit_solution(6118868752599392826)
XLA Ops:
  0.0 42.0 %shard_map.73 = (bf16[6,256,1152]{2,1,0:T(8,128)(2,1)}, bf16[6,256,256]{2,1,0:T(8,128)(2,1)}, bf16[6,256,256]{2,1,0:T(8,128)(2,1)}) custom-call(s32[12,6,16,352]{3,2,1,0:T(8,128)} %bitcast.2, s32[6,16,12]{2,1,0:T(8,128)} %bitcast.3, f32[6,256]{1,0:T(8,128)} %centers_ref.1, f32[6]{0:T(128)} %widths_ref.1), custom_call_target="tpu_custom_call" | custom-call | tf_op jit(solution)/shard_map/pallas_call | solution.py:304
  42.0 8.1 %shard_map.74 = bf16[12,6,88,256]{3,2,1,0:T(8,128)(2,1)} custom-call(bf16[6,256,1152]{2,1,0:T(8,128)(2,1)} %get-tuple-element.8.own_ref, bf16[6,256,256]{2,1,0:T(8,128)(2,1)} %get-tuple-element.9.top_ref, bf16[6,256,256]{2,1,0:T(8,128)(2,1)} %get-tuple-element.10.bottom_ref, bf16[4,264,768]{2,1,0:T(8,128)(2,1)} %constant.6.clone.mix_ref, ...), custom_call_target="tpu_custom_call" | custom-call | tf_op jit(solution)/shard_map/pallas_call | solution.py:347
